TPU v7x, 1024 devices: a whole 4x8x16 slice. The times are simulated.
1024 devices in a mesh: expert: 32 (over z, core), dp: 32 (over y, x).
Axes of the slice: x: 4, y: 8, z: 16, core: 2. Of those that a mesh axis runs over, the one named last changes fastest.
Arguments:
- out_grad: bfloat16 [32, 512, 2048], P('dp', 'expert'), may hold values from -200 to 200
- routes: int32 [32, 512, 8], P('dp', 'expert'), may hold values from 0 to 31, all different within a row; in each aligned block of 16 rows (0 to 15, 16 to 31, ..., all dimensions but the last counted through in order) at most 5 rows name the same one
- gate_probs: float32 [32, 512, 8], P('dp', 'expert'), may hold values from 0.1 to 0.6
- hidden: bfloat16 [32, 32, 160, 768], P('dp', 'expert'), may hold values from -60 to 60
- first_prev: float32 [32, 768, 2048], P('expert', 'dp'), may hold values from -0.125 to 0.125
- second_prev: float32 [32, 768, 2048], P('expert', 'dp'), may hold values from 1.2207031e-05 to 0.00012207031
Outputs:
- update: float32 [32, 768, 2048], P('expert', 'dp')
- lr_scale: float32 [32], P('expert')
Inputs may be any that keep to these rules, and one draw needn't show every extreme that they name: `routes`: each token names 8 different experts; among the 16 tokens of one device no expert is named more than 5 times.
All inputs are finite; a program needn't handle non-finite values.
Results may differ from a plain program's by a relative error of at most 0.0055.
Values may be sent and summed in bfloat16 or wider, within the bound.
A program may use at most 64 MiB of HBM per device.

v0:
```python
import jax
import jax.numpy as jnp
from jax import lax
from jax.sharding import PartitionSpec as P

PAD = 16
ADAM_STEP = 3


def dispatch_rows(tokens_here, chosen, weights_here, experts_all, capacity):
    onehot = (chosen[:, :, None] == jnp.arange(experts_all, dtype=jnp.int32)[None, None, :]).astype(
        jnp.float32
    )
    marked = jnp.sum(onehot, axis=1)
    earlier = jnp.cumsum(marked, axis=0) - marked
    scaled = jnp.sum(onehot * weights_here[:, :, None], axis=1)
    slot_ids = jnp.arange(capacity, dtype=jnp.float32)
    placing = scaled.T[:, None, :] * (earlier.T[:, None, :] == slot_ids[None, :, None]).astype(
        jnp.float32
    )
    outgoing = jnp.einsum(
        "ect,td->ecd", placing, tokens_here.astype(jnp.float32), precision=lax.Precision.HIGHEST
    ).astype(jnp.bfloat16)
    return (outgoing, jnp.sum(marked, axis=0))


def on_device(out_grad, routes, gate_probs, hidden, first_prev, second_prev):
    experts_all = lax.axis_size("expert")
    replicas = lax.axis_size("dp")
    saved_hidden = hidden[0, 0]
    slot_count = saved_hidden.shape[0]
    capacity = slot_count // experts_all
    outgoing, counted = dispatch_rows(out_grad[0], routes[0], gate_probs[0], experts_all, capacity)
    arrived, arrived_counts = (
        lax.all_to_all(outgoing, "expert", split_axis=0, concat_axis=0, tiled=True),
        lax.all_to_all(
            counted.astype(jnp.bfloat16), "expert", split_axis=0, concat_axis=0, tiled=True
        ),
    )
    model_width = arrived.shape[2]
    incoming = arrived.reshape(slot_count, model_width)
    saved_gram = lax.dot_general(
        saved_hidden, saved_hidden, (((1,), (1,)), ((), ())), preferred_element_type=jnp.float32
    )
    incoming_gram = lax.dot_general(
        incoming, incoming, (((1,), (1,)), ((), ())), preferred_element_type=jnp.float32
    )
    spread_local = jnp.sum(saved_gram * incoming_gram)
    routed = jnp.sum(arrived_counts.astype(jnp.int32))
    padded_rows = ((routed + PAD - 1) // PAD * PAD).astype(jnp.float32)
    spread_sum, total_rows = lax.psum((spread_local, padded_rows), "dp")
    gradient = lax.psum_scatter(
        lax.dot_general(
            saved_hidden, incoming, (((0,), (0,)), ((), ())), preferred_element_type=jnp.float32
        ).astype(jnp.bfloat16),
        "dp",
        scatter_dimension=0,
        tiled=True,
    ).astype(jnp.float32)
    power_local = jnp.sum(gradient * gradient)
    power_sum = lax.psum(power_local, "dp")
    noise_scale = total_rows * spread_sum / (replicas * power_sum + 1e-06)
    lr_scale = noise_scale / (noise_scale + total_rows / replicas)
    mean_grad = gradient / total_rows
    first_moment = 0.9 * first_prev[0] + 0.1 * mean_grad
    second_moment = 0.95 * second_prev[0] + 0.05 * mean_grad * mean_grad
    update = (
        -lr_scale
        * (first_moment / (1.0 - 0.9**ADAM_STEP))
        / (jnp.sqrt(second_moment / (1.0 - 0.95**ADAM_STEP)) + 1e-08)
    )
    return (update[None], lr_scale.reshape(1))


def solution(mesh):
    return jax.shard_map(
        on_device,
        mesh=mesh,
        in_specs=(
            P("dp", "expert", None),
            P("dp", "expert", None),
            P("dp", "expert", None),
            P("dp", "expert", None, None),
            P("expert", "dp", None),
            P("expert", "dp", None),
        ),
        out_specs=(P("expert", "dp", None), P("expert")),
        check_vma=False,
    )
```

profile of v0, /device:TPU:64, one launch (start us, length us, event | category | flops | bytes accessed | tf_op | source)
XLA Modules:
  0.0 405.1 jit_solution(5724132815545979437)
XLA Ops:
  7.2 0.0 copy-start
  7.2 0.0 reduce-scatter.4.cloned.1.call-start
  7.2 0.8 copy.33
  8.0 0.8 copy.34
  8.8 0.1 convert_reduce_fusion
  9.0 1.5 convolution_convert_fusion.1
  10.5 0.4 copy.35
  10.9 72.5 %all_to_all.11 = bf16[32,5,2048]{2,1,0:T(8,128)(2,1)S(1)} all-to-all(bf16[32,5,2048]{2,1,0:T(8,128)(2,1)S(1)} %copy.35), channel_id=1, replica_groups=mesh['expert'=32,'dp'=32] {'expert'}, dimensions={0} | all-to-all | bytes 1310720 | tf_op jit(solution)/shard_map/all_to_all | solution.py:35
  83.4 1.1 reshape.29
  84.5 0.0 copy-done
  84.5 2.1 fusion
  86.6 3.0 copy.38
  89.6 0.0 copy-start.1
  89.6 0.0 copy-start.2
  89.6 0.0 copy-start.3
  89.6 0.0 reduce-scatter.4.cloned.1.call-update
  89.6 0.1 copy.37
  89.7 16.2 %all_to_all.12 = bf16[32,1,1]{2,1,0:T(2,128)(2,1)S(1)} all-to-all(bf16[32,1,1]{2,1,0:T(2,128)(2,1)S(1)} %copy.37), channel_id=1, replica_groups=mesh['expert'=32,'dp'=32] {'expert'}, dimensions={0} | all-to-all | bytes 128 | tf_op jit(solution)/shard_map/all_to_all | solution.py:36
  105.9 0.7 convert_reduce_fusion.2
  107.3 0.0 copy-done.1
  107.3 0.3 fusion.18
  107.6 0.9 fusion.1
  108.5 208.9 %reduce-scatter.4.cloned.1.call-done = bf16[24,2048]{1,0:T(8,128)(2,1)} async-done(((bf16[768,2048]{1,0:T(8,128)(2,1)}), bf16[24,2048]{1,0:T(8,128)(2,1)}) %reduce-scatter.4.cloned.1.call-update) | async-done | bytes 98320 | tf_op jit(solution)/shard_map/reduce_scatter | solution.py:52
  317.4 1.5 fusion.4
  319.0 73.0 %all-reduce = (f32[]{:T(128)}, f32[]{:T(128)}, f32[]{:T(128)}) all-reduce(f32[]{:T(128)S(6)} %convert_element_type.45, f32[]{:T(128)} %fusion.1, f32[]{:T(128)} %fusion.4), channel_id=1, replica_groups=mesh['expert'=32,'dp'=32] {'dp'}, use_global_device_ids=true, to_apply=%region_6.7 | all-reduce | flops 3 | bytes 24 | tf_op jit(solution)/shard_map/psum | solution.py:51
  394.7 0.0 copy-done.2
  394.7 0.0 copy-done.3
  394.8 2.4 fusion.10
  (2 shorter events, 0.0 us)
Async XLA Ops:
  7.2 77.3 %copy-start = (bf16[1,1,160,768]{3,2,1,0:T(8,128)(2,1)S(1)}, bf16[1,1,160,768]{3,2,1,0:T(8,128)(2,1)}, u32[]{:S(2)}) copy-start(bf16[1,1,160,768]{3,2,1,0:T(8,128)(2,1)} %param.9) | copy-start | bytes 737284
  7.2 310.3 %reduce-scatter.4.cloned.1.call-start = ((), (), s32[]{:S(2)}) async-start(), calls=%async_computation.3 | async-start | bytes 3244032 | tf_op jit(solution)/shard_map/reduce_scatter | solution.py:52
  89.6 17.7 %copy-start.1 = (bf16[160,2048]{1,0:T(8,128)(2,1)S(1)}, bf16[160,2048]{1,0:T(8,128)(2,1)}, u32[]{:S(2)}) copy-start(bf16[160,2048]{1,0:T(8,128)(2,1)} %reshape.29) | copy-start | bytes 1966084
  89.6 305.1 %copy-start.2 = (f32[1,24,2048]{2,1,0:T(8,128)S(1)}, f32[1,24,2048]{2,1,0:T(8,128)}, u32[]{:S(2)}) copy-start(f32[1,24,2048]{2,1,0:T(8,128)} %param.11) | copy-start | bytes 589828
  89.6 305.1 %copy-start.3 = (f32[1,24,2048]{2,1,0:T(8,128)S(1)}, f32[1,24,2048]{2,1,0:T(8,128)}, u32[]{:S(2)}) copy-start(f32[1,24,2048]{2,1,0:T(8,128)} %param.10) | copy-start | bytes 589828
Sparse Core Ops, SparseCore 0:
  89.8 227.6 reduce-scatter.3
where the time goes:
time: 406 us; the launch traced here: 405 us
  waiting for transfers between devices  209 us (51%)
  blocking collectives  162 us (40%)
  between operations  18.7 us (5%)
  local copies, waits for them, and re-layouts  6.17 us (2%)
  matrix products  4.88 us (1%)
  other arithmetic  4.78 us (1%)
    reduce_scatter x1, waiting for transfers between devices, on_device(): lax.psum_scatter(lax.dot_general(saved_hidden, incoming, (((0,), (0,)), (...  209 us
    psum x1, blocking collectives, on_device(): spread_sum, total_rows = lax.psum((spread_local, padded_rows), 'dp')  73 us
    all_to_all x1, blocking collectives, on_device(): lax.all_to_all(outgoing, 'expert', split_axis=0, concat_axis=0, tiled=True)  72.5 us
    all_to_all x1, blocking collectives, on_device(): lax.all_to_all(counted.astype(jnp.bfloat16), 'expert', split_axis=0, conc...  16.2 us
  transfers between devices with their start and end apart: 1, of which 1 were waited for; matrix products, arithmetic and copies ran while one was open for 0% of the time, Pallas kernels for 0%

commit v1 on v0

v1 whole, which is shorter than its diff:
```python
import functools

import jax
import jax.numpy as jnp
from jax import lax
from jax.experimental import pallas as pl
from jax.experimental.pallas import tpu as pltpu
from jax.sharding import PartitionSpec as P

PAD = 16
ADAM_STEP = 3
MESH = pl.DeviceIdType.MESH
NX, NY, NZ = 4, 8, 16
HIGHEST = lax.Precision.HIGHEST
F32 = jnp.float32
BF16 = jnp.bfloat16


def iota(shape, dim):
    return lax.broadcasted_iota(jnp.int32, shape, dim)


def kernel(
    grads, routes, gates, hidden, first_prev, second_prev,
    out, lr_out,
    tok, info, info_x, hid, hid_t, sent, part, send_y, recv_y, own, relay, vec_x, vec_y, mom1, mom2,
    sem_local, sem_tok_x, sem_info_x, sem_hid, sem_send_x,
    sem_z, sem_z_info, sem_sib, sem_sib_info, sem_send_z, sem_send_zi,
    sem_send_y, sem_recv_y, sem_relay, sem_send_relay, sem_vx, sem_send_vx, sem_vy, sem_send_vy,
):
    expert = lax.axis_index("expert")
    dp = lax.axis_index("dp")
    z, core = expert // 2, expert % 2
    y, x = dp // NX, dp % NX
    top, tokens = routes.shape[1], routes.shape[2]
    width = grads.shape[2] // NX
    slots, hidden_units = hidden.shape[2], hidden.shape[3]
    owned = hidden_units // (NX * NY)
    block = owned * NX
    half = width // 2
    cap = slots // (2 * NZ)

    def at_x(k):
        return {"dp": y * NX + k}

    def at_y(k):
        return {"dp": k * NX + x}

    def at_z(k):
        return {"expert": k * 2 + core}

    sibling = {"expert": z * 2 + 1 - core}

    def remote(src, dst, send, recv, where):
        return pltpu.make_async_remote_copy(
            src_ref=src, dst_ref=dst, send_sem=send, recv_sem=recv, device_id=where, device_id_type=MESH
        )

    def columns(k):
        return pl.ds(pl.multiple_of(k * width, width), width)

    local_tok = pltpu.make_async_copy(
        grads.at[0, :, columns(x)],
        tok.at[core * NZ + z, pl.ds(pl.multiple_of(x * tokens, tokens), tokens)],
        sem_local.at[0],
    )
    local_tok.start()
    local_hid = pltpu.make_async_copy(
        hidden.at[0, 0], hid.at[pl.ds(pl.multiple_of(x * slots, slots), slots)], sem_local.at[1]
    )
    local_hid.start()
    local_m1 = pltpu.make_async_copy(first_prev.at[0], mom1, sem_local.at[2])
    local_m1.start()
    local_m2 = pltpu.make_async_copy(second_prev.at[0], mom2, sem_local.at[3])
    local_m2.start()

    barrier = pltpu.get_barrier_semaphore()
    for k in range(1, NX):
        pl.semaphore_signal(barrier, inc=1, device_id=at_x((x + k) % NX), device_id_type=MESH)
    for k in range(1, NY):
        pl.semaphore_signal(barrier, inc=1, device_id=at_y((y + k) % NY), device_id_type=MESH)
    for k in (1, NZ - 1):
        pl.semaphore_signal(barrier, inc=1, device_id=at_z((z + k) % NZ), device_id_type=MESH)
    pl.semaphore_signal(barrier, inc=1, device_id=sibling, device_id_type=MESH)

    lane = iota((tokens, 128), 1)
    token = iota((tokens, 128), 0)
    place_routes = (lane == x * tokens + token).astype(F32)
    place_gates = (lane == NX * tokens + x * tokens + token).astype(F32)
    info_x[x] = jnp.dot(routes[0].astype(F32), place_routes, preferred_element_type=F32) + jnp.dot(
        gates[0], place_gates, preferred_element_type=F32, precision=HIGHEST
    )
    pl.semaphore_wait(barrier, NX - 1 + NY - 1 + 3)

    here = core * NZ + z
    my_rows = pl.ds(pl.multiple_of(x * tokens, tokens), tokens)
    my_slots = pl.ds(pl.multiple_of(x * slots, slots), slots)
    x_copies = []
    for k in (1, 3, 2):
        peer = (x + k) % NX
        x_copies.append(remote(info_x.at[x], info_x.at[x], sem_send_x.at[0, k], sem_info_x.at[x], at_x(peer)))
        x_copies.append(
            remote(
                grads.at[0, :, columns(peer)], tok.at[here, my_rows], sem_send_x.at[1, k], sem_tok_x.at[x], at_x(peer)
            )
        )
    for copy in x_copies:
        copy.start()
    for k in (1, 3, 2):
        peer = (x + k) % NX
        copy = remote(hidden.at[0, 0], hid.at[my_slots], sem_send_x.at[2, k], sem_hid.at[x], at_x(peer))
        copy.start()
        x_copies.append(copy)

    def rows_of(i):
        return pl.ds(pl.multiple_of(((x + i) % NX) * tokens, tokens), tokens)

    def tok_copy(zz, i, where, recv):
        ref = tok.at[core * NZ + zz, rows_of(i)]
        return remote(ref, ref, sem_send_z, recv, where)

    def info_copy(zz, where, recv):
        ref = info.at[core * NZ + zz]
        return remote(ref, ref, sem_send_zi, recv, where)

    right, left = at_z((z + 1) % NZ), at_z((z + NZ - 1) % NZ)

    def send_tok(zz, i, to_right, to_left):
        if to_right:
            tok_copy(zz, i, right, sem_z.at[zz, i]).start()
        if to_left:
            tok_copy(zz, i, left, sem_z.at[zz, i]).start()
        tok_copy(zz, i, sibling, sem_sib).start()

    def send_info(zz, to_right, to_left):
        if to_right:
            info_copy(zz, right, sem_z_info.at[zz]).start()
        if to_left:
            info_copy(zz, left, sem_z_info.at[zz]).start()
        info_copy(zz, sibling, sem_sib_info).start()

    local_tok.wait()
    send_tok(z, 0, True, True)
    for k in (1, 3, 2):
        peer = (x + k) % NX
        remote(info_x.at[peer], info_x.at[peer], sem_send_x.at[0, k], sem_info_x.at[peer], at_x(peer)).wait_recv()
    info[here] = info_x[0] + info_x[1] + info_x[2] + info_x[3]
    send_info(z, True, True)
    for i in (1, 3, 2):
        peer = (x + i) % NX
        arrived = tok.at[here, rows_of(i)]
        remote(arrived, arrived, sem_send_x.at[1, i], sem_tok_x.at[peer], at_x(peer)).wait_recv()
        send_tok(z, i, True, True)

    order = (0, 1, 3, 2)

    def z_step(d, right_subs, left_subs, right_info, left_info, right_on, left_on, right_info_on, left_info_on):
        from_left = (z + NZ - d) % NZ
        from_right = (z + d) % NZ
        if right_info:
            info_copy(from_left, right, sem_z_info.at[from_left]).wait_recv()
            send_info(from_left, right_info_on, False)
        if left_info:
            info_copy(from_right, left, sem_z_info.at[from_right]).wait_recv()
            send_info(from_right, False, left_info_on)
        for i in order:
            if i in right_subs:
                tok_copy(from_left, i, right, sem_z.at[from_left, i]).wait_recv()
                send_tok(from_left, i, i in right_on, False)
            if i in left_subs:
                tok_copy(from_right, i, left, sem_z.at[from_right, i]).wait_recv()
                send_tok(from_right, i, False, i in left_on)

    def z_loop(d, carry):
        z_step(d, order, order, True, True, order, order, True, True)
        return carry

    lax.fori_loop(1, NZ // 2 - 1, z_loop, 0)
    z_step(NZ // 2 - 1, order, order, True, True, (0, 1), (3, 2), True, False)
    z_step(NZ // 2, (0, 1), (3, 2), True, False, (), (), False, False)

    local_hid.wait()
    for k in (1, 3, 2):
        peer = (x + k) % NX
        arrived = hid.at[pl.ds(pl.multiple_of(peer * slots, slots), slots)]
        remote(arrived, arrived, sem_send_x.at[2, k], sem_hid.at[peer], at_x(peer)).wait_recv()
    for k in range(NX * slots // 128):
        hid_t[:, 128 * k : 128 * (k + 1)] = hid[128 * k : 128 * (k + 1), :].T

    theirs = pl.ds(pl.multiple_of((1 - core) * NZ, NZ), NZ)
    remote(info.at[theirs], info.at[theirs], sem_send_zi, sem_sib_info, sibling).wait_recv()
    sources = 2 * NZ
    both = info[...]
    lanes3 = iota(both.shape, 2)
    hit = jnp.logical_and(both == expert.astype(F32), lanes3 < NX * tokens)
    weights = pltpu.roll(both.reshape(sources * top, 128), 128 - NX * tokens, 1).reshape(both.shape)
    named = jnp.sum(jnp.where(hit, 1.0, 0.0), axis=1)
    gate = jnp.sum(jnp.where(hit, weights, 0.0), axis=1)
    before_row, before_col = iota((128, 128), 0), iota((128, 128), 1)
    before = jnp.where(
        jnp.logical_and(before_row < before_col, before_row // tokens == before_col // tokens), 1.0, 0.0
    )
    place = jnp.dot(named.astype(BF16), before.astype(BF16), preferred_element_type=F32)
    row_of = iota(named.shape, 0)
    source = 2 * (row_of % NZ) + row_of // NZ
    target = jnp.where(named > 0.5, place + (cap * source).astype(F32), -1.0)
    count = jnp.sum(named, axis=0, keepdims=True)
    lane1 = iota(count.shape, 1)

    all_tokens = sources * tokens
    spread_row, spread_lane = iota((128, all_tokens), 0), iota((128, all_tokens), 1)
    own_row = iota((sources, all_tokens), 0) == iota((sources, all_tokens), 1) // tokens
    slot_id = iota((slots, all_tokens), 0).astype(F32)
    remote(tok.at[theirs], tok.at[theirs], sem_send_z, sem_sib, sibling).wait_recv()
    total = jnp.zeros((1, 1), F32)
    for r in range(NX):
        routed = jnp.sum(jnp.where(lane1 // tokens == r, count, 0.0), axis=1, keepdims=True)
        total = total + jnp.floor((routed + (PAD - 1.0)) * (1.0 / PAD)) * PAD
        repeat = jnp.where(spread_row == r * tokens + spread_lane % tokens, 1.0, 0.0)
        target_r = jnp.dot(target.astype(BF16), repeat.astype(BF16), preferred_element_type=F32)
        gate_r = jnp.dot(gate, repeat, preferred_element_type=F32, precision=HIGHEST)
        target_r = jnp.sum(jnp.where(own_row, target_r, 0.0), axis=0, keepdims=True)
        gate_r = jnp.sum(jnp.where(own_row, gate_r, 0.0), axis=0, keepdims=True)
        chosen = slot_id == target_r
        gate_col = jnp.sum(jnp.where(chosen, gate_r, 0.0), axis=1, keepdims=True)
        rows = tok[:, tokens * r : tokens * (r + 1), :].reshape(all_tokens, width)
        picked = jnp.dot(jnp.where(chosen, 1.0, 0.0).astype(BF16), rows, preferred_element_type=F32)
        sent[slots * r : slots * (r + 1), :] = (picked * gate_col).astype(BF16)

    up, down = at_y((y + 1) % NY), at_y((y + NY - 1) % NY)
    chains = ((0, 4), (0, 3), (1, 3), (1, 4))

    def block_of(k, h):
        return part[k, :, half * h : half * (h + 1)]

    def y_copy(c, k):
        return remote(
            send_y.at[c, k], recv_y.at[c, k], sem_send_y.at[c, k], sem_recv_y.at[c, k], down if c % 2 else up
        )

    def y_send(c, k):
        h, length = chains[c]
        far = length - k
        dest = (y + NY - far) % NY if c % 2 else (y + far) % NY
        value = block_of(dest, h)
        if k:
            y_copy(c, k - 1).wait_recv()
            value = value + recv_y[c, k - 1].astype(F32)
        send_y[c, k] = value.astype(BF16)
        y_copy(c, k).start()

    for h in range(2):
        part[:, :, half * h : half * (h + 1)] = jnp.dot(
            hid_t[...], sent[:, half * h : half * (h + 1)], preferred_element_type=F32
        ).reshape(NY, block, half)
        for c in (2 * h, 2 * h + 1):
            y_send(c, 0)
    spread = jnp.zeros((1, 1), F32)
    for r in range(NX):
        rows = pl.ds(slots * r, slots)
        over = (((1,), (1,)), ((), ()))
        gram_h = lax.dot_general(hid[rows, :], hid[rows, :], over, preferred_element_type=F32)
        gram_s = lax.dot_general(sent[rows, :], sent[rows, :], over, preferred_element_type=F32)
        both_grams = jnp.sum(gram_h * gram_s, axis=1, keepdims=True)
        spread = spread + jnp.sum(both_grams, axis=0, keepdims=True)
    for k in range(1, 4):
        for c in (0, 3, 1, 2):
            if k < chains[c][1]:
                y_send(c, k)
    for h in range(2):
        value = block_of(y, h)
        for c in (2 * h, 2 * h + 1):
            last = chains[c][1] - 1
            y_copy(c, last).wait_recv()
            value = value + recv_y[c, last].astype(F32)
        own[:, half * h : half * (h + 1)] = value

    relay_copies = []
    for k in (2, 1, 3):
        peer = (x + k) % NX
        rows = pl.ds(pl.multiple_of(peer * owned, 8), owned)
        copy = remote(own.at[rows], relay.at[x], sem_send_relay.at[k], sem_relay.at[x], at_x(peer))
        copy.start()
        relay_copies.append(copy)
    relay[x] = own[pl.ds(pl.multiple_of(x * owned, 8), owned), :]
    summed = own[...]
    power = jnp.sum(jnp.sum(summed * summed, axis=0, keepdims=True), axis=1, keepdims=True)
    sub = iota((8, 128), 0)
    vec_x[x] = jnp.where(
        sub == 0, power, jnp.where(sub == 1, spread, jnp.where(sub == 2, total * (1.0 / NX), 0.0))
    )
    for k in (2, 1, 3):
        copy = remote(vec_x.at[x], vec_x.at[x], sem_send_vx.at[k], sem_vx.at[x], at_x((x + k) % NX))
        copy.start()
        relay_copies.append(copy)
    for k in (1, 3, 2):
        peer = (x + k) % NX
        remote(vec_x.at[peer], vec_x.at[peer], sem_send_vx.at[k], sem_vx.at[peer], at_x(peer)).wait_recv()
    vec_y[y] = vec_x[0] + vec_x[1] + vec_x[2] + vec_x[3]
    for k in (4, 3, 5, 2, 6, 1, 7):
        copy = remote(vec_y.at[y], vec_y.at[y], sem_send_vy.at[k], sem_vy.at[y], at_y((y + k) % NY))
        copy.start()
        relay_copies.append(copy)
    local_m1.wait()
    local_m2.wait()
    for k in (1, 3, 2):
        peer = (x + k) % NX
        remote(relay.at[peer], relay.at[peer], sem_send_relay.at[k], sem_relay.at[peer], at_x(peer)).wait_recv()
    for k in range(1, NY):
        peer = (y + k) % NY
        remote(vec_y.at[peer], vec_y.at[peer], sem_send_vy.at[k], sem_vy.at[peer], at_y(peer)).wait_recv()
    scalars = vec_y[0]
    for k in range(1, NY):
        scalars = scalars + vec_y[k]
    power, spread, total = scalars[0:1, 0:1], scalars[1:2, 0:1], scalars[2:3, 0:1]
    replicas = float(NX * NY)
    noise = total * spread / (replicas * power + 1e-06)
    lr_scale = noise / (noise + total / replicas)
    lr_out[0] = lr_scale[0, 0]
    for k in range(NX):
        cols = pl.ds(width * k, width)
        mean = relay[k] / total
        first = 0.9 * mom1[:, cols] + 0.1 * mean
        second = 0.95 * mom2[:, cols] + 0.05 * mean * mean
        out[0, :, cols] = (
            -lr_scale
            * (first / (1.0 - 0.9**ADAM_STEP))
            / (jnp.sqrt(second / (1.0 - 0.95**ADAM_STEP)) + 1e-08)
        )

    for copy in x_copies + relay_copies:
        copy.wait_send()
    sent_blocks = tok.at[pl.ds(0, 31)]
    remote(sent_blocks, sent_blocks, sem_send_z, sem_sib, sibling).wait_send()
    sent_infos = info.at[pl.ds(0, 31)]
    remote(sent_infos, sent_infos, sem_send_zi, sem_sib_info, sibling).wait_send()
    for c in range(4):
        for k in range(chains[c][1]):
            y_copy(c, k).wait_send()


def on_device(out_grad, routes, gate_probs, hidden, first_prev, second_prev):
    routes = jnp.swapaxes(routes, 1, 2)
    gate_probs = jnp.swapaxes(gate_probs, 1, 2)
    tokens, width = out_grad.shape[1], out_grad.shape[2] // NX
    slots, units = hidden.shape[2:]
    owned = units // (NX * NY)
    block, half = owned * NX, width // 2
    dma = pltpu.SemaphoreType.DMA
    any_space = pl.BlockSpec(memory_space=pl.ANY)
    vmem = pl.BlockSpec(memory_space=pltpu.VMEM)
    return pl.pallas_call(
        kernel,
        out_shape=(
            jax.ShapeDtypeStruct(first_prev.shape, F32),
            jax.ShapeDtypeStruct((1,), F32),
        ),
        in_specs=[any_space, vmem, vmem, any_space, any_space, any_space],
        out_specs=(vmem, pl.BlockSpec(memory_space=pltpu.SMEM)),
        scratch_shapes=[
            pltpu.VMEM((2 * NZ, NX * tokens, width), BF16),
            pltpu.VMEM((2 * NZ, 8, 128), F32),
            pltpu.VMEM((NX, 8, 128), F32),
            pltpu.VMEM((NX * slots, units), BF16),
            pltpu.VMEM((units, NX * slots), BF16),
            pltpu.VMEM((NX * slots, width), BF16),
            pltpu.VMEM((NY, block, width), F32),
            pltpu.VMEM((4, 4, block, half), BF16),
            pltpu.VMEM((4, 4, block, half), BF16),
            pltpu.VMEM((block, width), F32),
            pltpu.VMEM((NX, owned, width), F32),
            pltpu.VMEM((NX, 8, 128), F32),
            pltpu.VMEM((NY, 8, 128), F32),
            pltpu.VMEM(first_prev.shape[1:], F32),
            pltpu.VMEM(first_prev.shape[1:], F32),
            dma((4,)),
            dma((NX,)),
            dma((NX,)),
            dma((NX,)),
            dma((3, NX)),
            dma((NZ, NX)),
            dma((NZ,)),
            dma,
            dma,
            dma,
            dma,
            dma((4, 4)),
            dma((4, 4)),
            dma((NX,)),
            dma((NX,)),
            dma((NX,)),
            dma((NX,)),
            dma((NY,)),
            dma((NY,)),
        ],
        compiler_params=pltpu.CompilerParams(
            collective_id=0, has_side_effects=True, vmem_limit_bytes=40 * 1024 * 1024
        ),
    )(out_grad, routes, gate_probs, hidden, first_prev, second_prev)


def solution(mesh):
    return jax.shard_map(
        on_device,
        mesh=mesh,
        in_specs=(
            P("dp", "expert", None),
            P("dp", "expert", None),
            P("dp", "expert", None),
            P("dp", "expert", None, None),
            P("expert", "dp", None),
            P("expert", "dp", None),
        ),
        out_specs=(P("expert", "dp", None), P("expert")),
        check_vma=False,
    )
```

time: 406 us -> 88.3 us (0.22)
  the two profiles are of different devices: /device:TPU:64 before, /device:TPU:6 now
where the time goes in v1:
time: 88.3 us; the launch traced here: 88 us
  Pallas kernels  79.8 us (90%)
  local copies, waits for them, and re-layouts  5.68 us (6%)
  between operations  2.47 us (3%)
    pallas_call x1, Pallas kernels, on_device(): pl.pallas_call(kernel, out_shape=(jax.ShapeDtypeStruct(first_prev.shape,...  79.8 us
    unnamed x13, local copies, waits for them, and re-layouts  5.68 us

profile of v1, /device:TPU:6, one launch (start us, length us, event | category | flops | bytes accessed | tf_op | source)
XLA Modules:
  0.0 88.0 jit_solution(9617031428674468934)
XLA Ops:
  0.6 0.0 copy-start
  0.6 0.9 %copy-done = bf16[1,1,160,768]{3,2,1,0:T(8,128)(2,1)S(1)} copy-done((bf16[1,1,160,768]{3,2,1,0:T(8,128)(2,1)S(1)}, bf16[1,1,160,768]{3,2,1,0:T(8,128)(2,1)}, u32[]{:S(2)}) %copy-start) | copy-done | bytes 245784
  1.6 0.0 copy-start.1
  1.6 0.9 %copy-done.1 = f32[1,24,2048]{2,1,0:T(8,128)S(1)} copy-done((f32[1,24,2048]{2,1,0:T(8,128)S(1)}, f32[1,24,2048]{2,1,0:T(8,128)}, u32[]{:S(2)}) %copy-start.1) | copy-done | bytes 196632
  2.5 0.0 copy-start.2
  2.5 0.9 %copy-done.2 = f32[1,24,2048]{2,1,0:T(8,128)S(1)} copy-done((f32[1,24,2048]{2,1,0:T(8,128)S(1)}, f32[1,24,2048]{2,1,0:T(8,128)}, u32[]{:S(2)}) %copy-start.2) | copy-done | bytes 196632
  3.4 0.0 copy-start.3
  3.4 0.8 copy-done.3
  4.3 0.0 copy-start.4
  4.3 0.7 copy-done.4
  5.0 0.0 copy-start.5
  5.0 0.7 copy-done.5
  5.6 79.8 %shard_map.77 = (f32[1,24,2048]{2,1,0:T(8,128)S(1)}, f32[1]{0:T(128)}) custom-call(bf16[1,16,2048]{2,1,0:T(8,128)(2,1)S(1)} %copy-done.3, s32[1,8,16]{2,1,0:T(8,128)S(1)} %bitcast.2, f32[1,8,16]{2,1,0:T(8,128)S(1)} %bitcast.3, bf16[1,1,160,768]{3,2,1,0:T(8,128)(2,1)S(1)} %copy-done, f32[1,24,2048]{2,1,0:T(8,128)S(1)} %copy-done.1, f32[1,24,2048]{2,1,0:T(8,128)S(1)} %copy-done.2), custom_call_target="tpu_custom_call" | custom-call | tf_op jit(solution)/shard_map/pallas_call | solution.py:352
  85.5 0.7 copy.10
Async XLA Ops:
  0.6 0.9 %copy-start = (bf16[1,1,160,768]{3,2,1,0:T(8,128)(2,1)S(1)}, bf16[1,1,160,768]{3,2,1,0:T(8,128)(2,1)}, u32[]{:S(2)}) copy-start(bf16[1,1,160,768]{3,2,1,0:T(8,128)(2,1)} %hidden.1) | copy-start | bytes 737284
  1.6 0.9 %copy-start.1 = (f32[1,24,2048]{2,1,0:T(8,128)S(1)}, f32[1,24,2048]{2,1,0:T(8,128)}, u32[]{:S(2)}) copy-start(f32[1,24,2048]{2,1,0:T(8,128)} %first_prev.1) | copy-start | bytes 589828
  2.5 0.9 %copy-start.2 = (f32[1,24,2048]{2,1,0:T(8,128)S(1)}, f32[1,24,2048]{2,1,0:T(8,128)}, u32[]{:S(2)}) copy-start(f32[1,24,2048]{2,1,0:T(8,128)} %second_prev.1) | copy-start | bytes 589828
  3.4 0.8 copy-start.3
  4.3 0.7 copy-start.4
  5.0 0.7 copy-start.5

commit v2 on v0

v2 whole, which is shorter than its diff:
```python
import jax
import jax.numpy as jnp
from jax import lax
from jax.experimental import pallas as pl
from jax.experimental.pallas import tpu as pltpu
from jax.sharding import PartitionSpec as P

PAD = 16
ADAM_STEP = 3
MESH = pl.DeviceIdType.MESH
NX, NY, NZ = 4, 8, 16
HIGHEST = lax.Precision.HIGHEST
F32 = jnp.float32
BF16 = jnp.bfloat16


def iota(shape, dim):
    return lax.broadcasted_iota(jnp.int32, shape, dim)


def kernel(
    grads, routes_in, gates_in, hidden, first_prev, second_prev,
    out, lr_out,
    tok, info, info_y, info_own, hid, hid_pass, hid_t, sent, part, send_x, recv_x, own, relay, vec, mom1, mom2,
    routes, gates,
    sem_local, sem_tok, sem_send_tok, sem_info, sem_send_info,
    sem_z, sem_z_info, sem_send_z, sem_send_zi, sem_sib, sem_sib_info, sem_send_sib, sem_send_sibi,
    sem_hand, sem_send_hand, sem_h, sem_send_h, sem_sib_h, sem_send_sib_h,
    sem_x, sem_send_x, sem_relay, sem_send_relay, sem_vec, sem_send_vec,
):
    expert = lax.axis_index("expert")
    dp = lax.axis_index("dp")
    z, core = expert // 2, expert % 2
    y, x = dp // NX, dp % NX
    tokens = routes_in.shape[2]
    width = grads.shape[2] // NY
    slots, units = hidden.shape[2], hidden.shape[3]
    owned = units // (NX * NY)
    cap = slots // (2 * NZ)
    sources = 2 * NZ
    all_tokens = sources * tokens
    quarter = NY * tokens // 2
    half = slots // 2

    def at_x(k):
        return {"dp": y * NX + k}

    def at_y(k):
        return {"dp": k * NX + x}

    def at_z(k):
        return {"expert": k * 2 + core}

    def core1_at_y(k):
        return {"expert": z * 2 + 1, "dp": k * NX + x}

    sibling = {"expert": z * 2 + 1 - core}

    def remote(src, dst, send, recv, where):
        return pltpu.make_async_remote_copy(
            src_ref=src, dst_ref=dst, send_sem=send, recv_sem=recv, device_id=where, device_id_type=MESH
        )

    def arrived(ref, sem):
        remote(ref, ref, sem_send_hand, sem, sibling).wait_recv()

    def left(ref, sem):
        remote(ref, ref, sem, sem_hand, sibling).wait_send()

    def columns(k):
        return pl.ds(pl.multiple_of(k * width, width), width)

    def rows(k, count):
        return pl.ds(pl.multiple_of(k * count, count), count)

    local = [
        pltpu.make_async_copy(routes_in, routes, sem_local.at[0]),
        pltpu.make_async_copy(gates_in, gates, sem_local.at[1]),
        pltpu.make_async_copy(hidden.at[0, 0], hid.at[y], sem_local.at[2]),
        pltpu.make_async_copy(first_prev.at[0], mom1, sem_local.at[3]),
        pltpu.make_async_copy(second_prev.at[0], mom2, sem_local.at[4]),
    ]
    for copy in local:
        copy.start()

    barrier = pltpu.get_barrier_semaphore()

    def greet(where):
        pl.semaphore_signal(barrier, inc=1, device_id=where, device_id_type=MESH)

    greet(sibling)
    for k in range(1, NY):
        greet({"expert": z * 2 + 1 - core, "dp": ((y + k) % NY) * NX + x})
    for k in range(1, NX * NY):
        greet({"dp": (dp + k) % (NX * NY)})

    @pl.when(core == 1)
    def _():
        greet(at_z((z + 1) % NZ))
        greet(at_z((z + NZ - 1) % NZ))
        pl.semaphore_wait(barrier, NX * NY - 1 + NY + 2)

    @pl.when(core == 0)
    def _():
        pl.semaphore_wait(barrier, NX * NY - 1 + NY)

    my_rows = rows(y, tokens)
    for k in range(1, NY):
        peer = (y + k) % NY
        remote(
            grads.at[0, :, columns(peer)], tok.at[expert, my_rows], sem_send_tok, sem_tok.at[core, y // 4],
            core1_at_y(peer),
        ).start()

    @pl.when(core == 0)
    def _():
        remote(
            grads.at[0, :, columns(y)], tok.at[expert, my_rows], sem_send_tok, sem_tok.at[core, y // 4], sibling
        ).start()

    @pl.when(core == 1)
    def _():
        pltpu.make_async_copy(grads.at[0, :, columns(y)], tok.at[expert, my_rows], sem_tok.at[core, y // 4]).start()
        remote(hidden.at[0, 0], hid_pass.at[y], sem_send_hand, sem_hand, sibling).start()

    up, down = at_y((y + 1) % NY), at_y((y + NY - 1) % NY)

    def hid_copy(e, r, h, where, first=False):
        held = hid_pass if e else hid
        ref = held.at[r, pl.ds(half * h, half)]
        src = hidden.at[0, 0, pl.ds(half * h, half)] if first and not e else ref
        return remote(src, ref, sem_send_h.at[e], sem_h.at[r, e, h], where)

    @pl.when(core == 0)
    def _():
        for h in range(2):
            hid_copy(0, y, h, up, True).start()
            hid_copy(0, y, h, down, True).start()

    place_lanes = (iota((tokens, 128), 1) == y * tokens + iota((tokens, 128), 0)).astype(F32)
    local[0].wait()
    local[1].wait()
    info_own[0:8] = jnp.dot(routes[0].astype(F32), place_lanes, preferred_element_type=F32)
    info_own[8:16] = jnp.dot(gates[0], place_lanes, preferred_element_type=F32, precision=HIGHEST)
    mine = core * NY + y
    for k in range(1, NY):
        remote(info_own, info_y.at[mine], sem_send_info, sem_info, core1_at_y((y + k) % NY)).start()

    @pl.when(core == 0)
    def _():
        remote(info_own, info_y.at[mine], sem_send_info, sem_info, sibling).start()

        def hand_over(r, h):
            ref = hid_pass.at[r, pl.ds(half * h, half)]
            remote(ref, hid.at[r, pl.ds(half * h, half)], sem_send_sib_h, sem_sib_h, sibling).start()

        arrived(hid_pass.at[y], sem_hand)
        for h in range(2):
            hid_copy(1, y, h, up).start()
            hid_copy(1, y, h, down).start()
        for d in range(1, 5):
            below, above = (y + NY - d) % NY, (y + d) % NY
            for e in range(2):
                for h in range(2):
                    if d < 4 or e == 0:
                        hid_copy(e, below, h, up).wait_recv()
                        if d < 3 or (d == 3 and e == 0):
                            hid_copy(e, below, h, up).start()
                        if e == 1:
                            hand_over(below, h)
                    if d < 4 or e == 1:
                        hid_copy(e, above, h, down).wait_recv()
                        if d < 3 or (d == 3 and e == 1):
                            hid_copy(e, above, h, down).start()
                        if e == 1:
                            hand_over(above, h)
        local[2].wait()

    subs = ((1, 0), (1, 1), (0, 0), (0, 1))

    @pl.when(core == 1)
    def _():
        right, left_ = at_z((z + 1) % NZ), at_z((z + NZ - 1) % NZ)

        def tok_ref(zz, c, h):
            return tok.at[2 * zz + c, pl.ds(quarter * h, quarter)]

        def tok_copy(zz, c, h, where):
            ref = tok_ref(zz, c, h)
            return remote(ref, ref, sem_send_z, sem_z.at[zz, 2 * c + h], where)

        def tok_share(zz, c, h):
            ref = tok_ref(zz, c, h)
            remote(ref, ref, sem_send_sib, sem_sib, sibling).start()

        def info_ref(zz):
            return info.at[pl.ds(pl.multiple_of(2 * zz, 2), 2)]

        def info_copy(zz, where):
            return remote(info_ref(zz), info_ref(zz), sem_send_zi, sem_z_info.at[zz], where)

        def info_share(zz):
            remote(info_ref(zz), info_ref(zz), sem_send_sibi, sem_sib_info, sibling).start()

        for c, h in subs:
            arrived(tok_ref(z, c, h), sem_tok.at[c, h])
            tok_copy(z, c, h, right).start()
            tok_copy(z, c, h, left_).start()
            tok_share(z, c, h)
        arrived(info_y.at[pl.ds(0, 2 * NY - 1)], sem_info)
        info_y[mine] = info_own[...]
        for c in range(2):
            total_info = info_y[c * NY]
            for k in range(1, NY):
                total_info = total_info + info_y[c * NY + k]
            info[2 * z + c] = total_info
        info_copy(z, right).start()
        info_copy(z, left_).start()
        info_share(z)

        def z_step(d, last):
            from_left, from_right = (z + NZ - d) % NZ, (z + d) % NZ
            for c, h in subs:
                if last < 2 or c == 1:
                    tok_copy(from_left, c, h, right).wait_recv()
                    if last == 0 or (last == 1 and c == 1):
                        tok_copy(from_left, c, h, right).start()
                    tok_share(from_left, c, h)
                if last < 2 or c == 0:
                    tok_copy(from_right, c, h, left_).wait_recv()
                    if last == 0 or (last == 1 and c == 0):
                        tok_copy(from_right, c, h, left_).start()
                    tok_share(from_right, c, h)
            info_copy(from_left, right).wait_recv()
            if last < 2:
                info_copy(from_left, right).start()
            info_share(from_left)
            if last < 2:
                info_copy(from_right, left_).wait_recv()
                if last == 0:
                    info_copy(from_right, left_).start()
                info_share(from_right)

        def z_loop(d, carry):
            z_step(d, 0)
            return carry

        lax.fori_loop(1, NZ // 2 - 1, z_loop, 0)
        z_step(NZ // 2 - 1, 1)
        z_step(NZ // 2, 2)
        local[2].wait()
        arrived(hid.at[pl.ds(0, NY - 1)], sem_sib_h)

    for k in range(NY * slots // 128):
        first, last = 128 * k // slots, (128 * k + 127) // slots
        begin = 128 * k - first * slots
        if first == last:
            piece = hid[first, begin : begin + 128, :]
        else:
            cut = slots - begin
            piece = jnp.concatenate([hid[first, begin:slots, :], hid[last, 0 : 128 - cut, :]], axis=0)
        hid_t[:, 128 * k : 128 * (k + 1)] = piece.T

    @pl.when(core == 0)
    def _():
        arrived(info, sem_sib_info)

    both = info[...]
    hit = both[:, 0:8, :] == expert.astype(F32)
    named = jnp.sum(jnp.where(hit, 1.0, 0.0), axis=1)
    gate = jnp.sum(jnp.where(hit, both[:, 8:16, :], 0.0), axis=1)
    from_row, to_col = iota((128, 128), 0), iota((128, 128), 1)
    same = from_row // tokens == to_col // tokens
    before = jnp.where(jnp.logical_and(same, from_row < to_col), 1.0, 0.0).astype(BF16)
    place = jnp.dot(named.astype(BF16), before, preferred_element_type=F32)
    target = jnp.where(named > 0.5, place + (cap * iota(named.shape, 0)).astype(F32), -1.0).astype(BF16)
    count = jnp.sum(named, axis=0, keepdims=True)
    routed = jnp.dot(
        jnp.broadcast_to(count, (8, 128)).astype(BF16), jnp.where(same, 1.0, 0.0).astype(BF16),
        preferred_element_type=F32,
    )[0:1]
    padded = jnp.floor((routed + (PAD - 1.0)) * (1.0 / PAD)) * PAD
    total = jnp.sum(padded, axis=1, keepdims=True) * (1.0 / tokens)

    lane_row, lane_col = iota((128, all_tokens), 0), iota((128, all_tokens), 1)
    own_row = iota((sources, all_tokens), 0) == iota((sources, all_tokens), 1) // tokens
    slot_id = iota((slots, all_tokens), 0).astype(F32)

    @pl.when(core == 0)
    def _():
        arrived(tok, sem_sib)

    for r in range(NY):
        repeat = jnp.where(lane_row == r * tokens + lane_col % tokens, 1.0, 0.0)
        target_r = jnp.dot(target, repeat.astype(BF16), preferred_element_type=F32)
        gate_r = jnp.dot(gate, repeat, preferred_element_type=F32, precision=HIGHEST)
        target_r = jnp.sum(jnp.where(own_row, target_r, 0.0), axis=0, keepdims=True)
        gate_r = jnp.sum(jnp.where(own_row, gate_r, 0.0), axis=0, keepdims=True)
        chosen = slot_id == target_r
        gate_col = jnp.sum(jnp.where(chosen, gate_r, 0.0), axis=1, keepdims=True)
        block = tok[:, tokens * r : tokens * (r + 1), :].reshape(all_tokens, width)
        picked = jnp.dot(jnp.where(chosen, 1.0, 0.0).astype(BF16), block, preferred_element_type=F32)
        sent[slots * r : slots * (r + 1), :] = (picked * gate_col).astype(BF16)

    part[...] = jnp.dot(hid_t[...], sent[...], preferred_element_type=F32).reshape(NY, NX, owned, width)
    for k in (2, 1, 3):
        peer = (x + k) % NX
        send_x[peer] = part[:, peer].reshape(NY * owned, width).astype(BF16)
        remote(send_x.at[peer], recv_x.at[x], sem_send_x.at[k], sem_x.at[x], at_x(peer)).start()

    over = (((1,), (1,)), ((), ()))
    spread = jnp.zeros((1, 1), F32)
    for r in range(NY):
        sent_r = sent[slots * r : slots * (r + 1), :]
        gram_h = lax.dot_general(hid[r], hid[r], over, preferred_element_type=F32)
        gram_s = lax.dot_general(sent_r, sent_r, over, preferred_element_type=F32)
        both_grams = jnp.sum(gram_h * gram_s, axis=0, keepdims=True)
        spread = spread + jnp.sum(both_grams, axis=1, keepdims=True)

    summed = part[:, x].reshape(NY * owned, width)
    for k in (1, 3, 2):
        peer = (x + k) % NX
        arrived(recv_x.at[peer], sem_x.at[peer])
        summed = summed + recv_x[peer].astype(F32)
    own[...] = summed

    power = jnp.sum(jnp.sum(summed * summed, axis=0, keepdims=True), axis=1, keepdims=True)
    sub = iota((8, 128), 0)
    vec[dp] = jnp.where(
        sub == 0, power, jnp.where(sub == 1, spread, jnp.where(sub == 2, total * (1.0 / NY), 0.0))
    )
    for k in (4, 3, 5, 2, 6, 1, 7):
        for i in range(NX):
            peer = ((y + k) % NY) * NX + (x + i) % NX
            remote(vec.at[dp], vec.at[dp], sem_send_vec, sem_vec, {"dp": peer}).start()
    for i in range(1, NX):
        remote(vec.at[dp], vec.at[dp], sem_send_vec, sem_vec, at_x((x + i) % NX)).start()
    for k in (4, 3, 5, 2, 6, 1, 7):
        peer = (y + k) % NY
        remote(own.at[rows(peer, owned)], relay.at[y], sem_send_relay, sem_relay, at_y(peer)).start()
    relay[y] = own[rows(y, owned), :]
    local[3].wait()
    local[4].wait()
    arrived(relay.at[pl.ds(0, NY - 1)], sem_relay)
    arrived(vec.at[pl.ds(0, NX * NY - 1)], sem_vec)
    scalars = vec[0]
    for k in range(1, NX * NY):
        scalars = scalars + vec[k]
    power, spread, total = scalars[0:1, 0:1], scalars[1:2, 0:1], scalars[2:3, 0:1]
    replicas = float(NX * NY)
    noise = total * spread / (replicas * power + 1e-06)
    lr_scale = noise / (noise + total / replicas)
    lr_out[0] = lr_scale[0, 0]
    for k in range(NY):
        cols = pl.ds(width * k, width)
        mean = relay[k] / total
        first = 0.9 * mom1[:, cols] + 0.1 * mean
        second = 0.95 * mom2[:, cols] + 0.05 * mean * mean
        out[0, :, cols] = (
            -lr_scale
            * (first / (1.0 - 0.9**ADAM_STEP))
            / (jnp.sqrt(second / (1.0 - 0.95**ADAM_STEP)) + 1e-08)
        )

    tok_flat = tok.at[0, pl.ds(0, tokens * (NY - 1))]
    left(tok_flat, sem_send_tok)
    left(info_y.at[pl.ds(0, NY - 1)], sem_send_info)
    for k in (2, 1, 3):
        left(send_x.at[(x + k) % NX], sem_send_x.at[k])
    left(relay.at[pl.ds(0, NY - 1)], sem_send_relay)
    left(vec.at[pl.ds(0, NX * NY - 1)], sem_send_vec)

    @pl.when(core == 0)
    def _():
        left(tok.at[0, pl.ds(0, tokens)], sem_send_tok)
        left(info_y.at[0], sem_send_info)
        for e in range(2):
            left(hid.at[pl.ds(0, NY - 1)], sem_send_h.at[e])
        left(hid.at[pl.ds(0, NY - 1)], sem_send_sib_h)

    @pl.when(core == 1)
    def _():
        left(hid.at[0], sem_send_hand)
        left(tok.at[pl.ds(0, 30)], sem_send_z)
        left(tok, sem_send_sib)
        left(info.at[pl.ds(0, 30)], sem_send_zi)
        left(info, sem_send_sibi)


def on_device(out_grad, routes, gate_probs, hidden, first_prev, second_prev):
    routes = jnp.swapaxes(routes, 1, 2)
    gate_probs = jnp.swapaxes(gate_probs, 1, 2)
    tokens, width = out_grad.shape[1], out_grad.shape[2] // NY
    slots, units = hidden.shape[2:]
    owned = units // (NX * NY)
    dma = pltpu.SemaphoreType.DMA
    hbm = pl.BlockSpec(memory_space=pltpu.HBM)
    vmem = pl.BlockSpec(memory_space=pltpu.VMEM)
    return pl.pallas_call(
        kernel,
        out_shape=(
            jax.ShapeDtypeStruct(first_prev.shape, F32),
            jax.ShapeDtypeStruct((1,), F32),
        ),
        in_specs=[hbm] * 6,
        out_specs=(vmem, pl.BlockSpec(memory_space=pltpu.SMEM)),
        scratch_shapes=[
            pltpu.VMEM((2 * NZ, NY * tokens, width), BF16),
            pltpu.VMEM((2 * NZ, 16, 128), F32),
            pltpu.VMEM((2 * NY, 16, 128), F32),
            pltpu.VMEM((16, 128), F32),
            pltpu.VMEM((NY, slots, units), BF16),
            pltpu.VMEM((NY, slots, units), BF16),
            pltpu.VMEM((units, NY * slots), BF16),
            pltpu.VMEM((NY * slots, width), BF16),
            pltpu.VMEM((NY, NX, owned, width), F32),
            pltpu.VMEM((NX, NY * owned, width), BF16),
            pltpu.VMEM((NX, NY * owned, width), BF16),
            pltpu.VMEM((NY * owned, width), F32),
            pltpu.VMEM((NY, owned, width), F32),
            pltpu.VMEM((NX * NY, 8, 128), F32),
            pltpu.VMEM(first_prev.shape[1:], F32),
            pltpu.VMEM(first_prev.shape[1:], F32),
            pltpu.VMEM(routes.shape, jnp.int32),
            pltpu.VMEM(routes.shape, F32),
            dma((5,)),
            dma((2, 2)),
            dma,
            dma,
            dma,
            dma((NZ, 4)),
            dma((NZ,)),
            dma,
            dma,
            dma,
            dma,
            dma,
            dma,
            dma,
            dma,
            dma((NY, 2, 2)),
            dma((2,)),
            dma,
            dma,
            dma((NX,)),
            dma((NX,)),
            dma,
            dma,
            dma,
            dma,
        ],
        compiler_params=pltpu.CompilerParams(
            collective_id=0, has_side_effects=True, vmem_limit_bytes=60 * 1024 * 1024
        ),
    )(out_grad, routes, gate_probs, hidden, first_prev, second_prev)


def solution(mesh):
    return jax.shard_map(
        on_device,
        mesh=mesh,
        in_specs=(
            P("dp", "expert", None),
            P("dp", "expert", None),
            P("dp", "expert", None),
            P("dp", "expert", None, None),
            P("expert", "dp", None),
            P("expert", "dp", None),
        ),
        out_specs=(P("expert", "dp", None), P("expert")),
        check_vma=False,
    )
```

time: 406 us -> 78 us (0.19)
  the two profiles are of different devices: /device:TPU:64 before, /device:TPU:1 now
where the time goes in v2:
time: 78 us; the launch traced here: 77.8 us
  Pallas kernels  73.8 us (95%)
  between operations  2.4 us (3%)
  local copies, waits for them, and re-layouts  1.62 us (2%)
    pallas_call x1, Pallas kernels, on_device(): pl.pallas_call(kernel, out_shape=(jax.ShapeDtypeStruct(first_prev.shape,...  73.8 us
    unnamed x1, local copies, waits for them, and re-layouts  1.62 us

profile of v2, /device:TPU:1, one launch (start us, length us, event | category | flops | bytes accessed | tf_op | source)
XLA Modules:
  0.0 77.8 jit_solution(144158562510095351)
XLA Ops:
  0.6 73.8 %shard_map.77 = (f32[1,24,2048]{2,1,0:T(8,128)}, f32[1]{0:T(128)}) custom-call(bf16[1,16,2048]{2,1,0:T(8,128)(2,1)} %grads.1, s32[1,8,16]{2,1,0:T(8,128)} %bitcast.2, f32[1,8,16]{2,1,0:T(8,128)} %bitcast.3, bf16[1,1,160,768]{3,2,1,0:T(8,128)(2,1)} %hidden.1, f32[1,24,2048]{2,1,0:T(8,128)} %first_prev.1, f32[1,24,2048]{2,1,0:T(8,128)} %second_prev.1), custom_call_target="tpu_custom_call" | custom-call | tf_op jit(solution)/shard_map/pallas_call | solution.py:399
  74.4 1.6 %copy.10 = f32[1,24,2048]{2,1,0:T(8,128)} copy(f32[1,24,2048]{2,1,0:T(8,128)} %get-tuple-element.4) | data formatting | bytes 393216

commit v3 on v2

--- a/solution.py
+++ b/solution.py
@@ -9,6 +9,9 @@
 ADAM_STEP = 3
 MESH = pl.DeviceIdType.MESH
 NX, NY, NZ = 4, 8, 16
+REACH = NZ // 2
+HOPS = {0: (2, 1), 2: (2, 1), 4: (2, 1), 6: (2, 1)}
+ORDER = (2, 1, 4, 3, 6, 5, 8, 7)
 HIGHEST = lax.Precision.HIGHEST
 F32 = jnp.float32
 BF16 = jnp.bfloat16
@@ -21,12 +24,12 @@
 def kernel(
     grads, routes_in, gates_in, hidden, first_prev, second_prev,
     out, lr_out,
-    tok, info, info_y, info_own, hid, hid_pass, hid_t, sent, part, send_x, recv_x, own, relay, vec, mom1, mom2,
+    tok, info, info_y, info_own, grads_here, hid, hid_pass, hid_t, sent, part, send_x, recv_x, own, relay, vec, norms, mom1, mom2,
     routes, gates,
     sem_local, sem_tok, sem_send_tok, sem_info, sem_send_info,
     sem_z, sem_z_info, sem_send_z, sem_send_zi, sem_sib, sem_sib_info, sem_send_sib, sem_send_sibi,
     sem_hand, sem_send_hand, sem_h, sem_send_h, sem_sib_h, sem_send_sib_h,
-    sem_x, sem_send_x, sem_relay, sem_send_relay, sem_vec, sem_send_vec,
+    sem_x, sem_send_x, sem_relay, sem_send_relay, sem_vec, sem_send_vec, sem_norms, sem_send_norms,
 ):
     expert = lax.axis_index("expert")
     dp = lax.axis_index("dp")
@@ -79,6 +82,7 @@
         pltpu.make_async_copy(hidden.at[0, 0], hid.at[y], sem_local.at[2]),
         pltpu.make_async_copy(first_prev.at[0], mom1, sem_local.at[3]),
         pltpu.make_async_copy(second_prev.at[0], mom2, sem_local.at[4]),
+        pltpu.make_async_copy(grads.at[0], grads_here, sem_local.at[5]),
     ]
     for copy in local:
         copy.start()
@@ -96,31 +100,45 @@
 
     @pl.when(core == 1)
     def _():
-        greet(at_z((z + 1) % NZ))
-        greet(at_z((z + NZ - 1) % NZ))
-        pl.semaphore_wait(barrier, NX * NY - 1 + NY + 2)
+        for k in (1, 2, NZ - 2, NZ - 1):
+            greet(at_z((z + k) % NZ))
+
+    lane_of = iota((tokens, 128), 1) % tokens == iota((tokens, 128), 0)
+    spread_out = jnp.where(lane_of, 1.0, 0.0)
+    choice = iota((8, 128), 0) == iota((8, 128), 1) // tokens
+    local[0].wait()
+    local[1].wait()
+    wide = jnp.dot(routes[0].astype(F32), spread_out, preferred_element_type=F32)
+    info_own[0:1] = jnp.sum(jnp.where(choice, wide, 0.0), axis=0, keepdims=True)
+    wide = jnp.dot(gates[0], spread_out, preferred_element_type=F32, precision=HIGHEST)
+    info_own[1:2] = jnp.sum(jnp.where(choice, wide, 0.0), axis=0, keepdims=True)
+
+    @pl.when(core == 1)
+    def _():
+        pl.semaphore_wait(barrier, NX * NY - 1 + NY + 4)
 
     @pl.when(core == 0)
     def _():
         pl.semaphore_wait(barrier, NX * NY - 1 + NY)
 
     my_rows = rows(y, tokens)
+    local[5].wait()
     for k in range(1, NY):
         peer = (y + k) % NY
         remote(
-            grads.at[0, :, columns(peer)], tok.at[expert, my_rows], sem_send_tok, sem_tok.at[core, y // 4],
+            grads_here.at[:, columns(peer)], tok.at[expert, my_rows], sem_send_tok, sem_tok.at[core, y // 4],
             core1_at_y(peer),
         ).start()
 
     @pl.when(core == 0)
     def _():
         remote(
-            grads.at[0, :, columns(y)], tok.at[expert, my_rows], sem_send_tok, sem_tok.at[core, y // 4], sibling
+            grads_here.at[:, columns(y)], tok.at[expert, my_rows], sem_send_tok, sem_tok.at[core, y // 4], sibling
         ).start()
 
     @pl.when(core == 1)
     def _():
-        pltpu.make_async_copy(grads.at[0, :, columns(y)], tok.at[expert, my_rows], sem_tok.at[core, y // 4]).start()
+        pltpu.make_async_copy(grads_here.at[:, columns(y)], tok.at[expert, my_rows], sem_tok.at[core, y // 4]).start()
         remote(hidden.at[0, 0], hid_pass.at[y], sem_send_hand, sem_hand, sibling).start()
 
     up, down = at_y((y + 1) % NY), at_y((y + NY - 1) % NY)
@@ -137,18 +155,12 @@
             hid_copy(0, y, h, up, True).start()
             hid_copy(0, y, h, down, True).start()
 
-    place_lanes = (iota((tokens, 128), 1) == y * tokens + iota((tokens, 128), 0)).astype(F32)
-    local[0].wait()
-    local[1].wait()
-    info_own[0:8] = jnp.dot(routes[0].astype(F32), place_lanes, preferred_element_type=F32)
-    info_own[8:16] = jnp.dot(gates[0], place_lanes, preferred_element_type=F32, precision=HIGHEST)
-    mine = core * NY + y
     for k in range(1, NY):
-        remote(info_own, info_y.at[mine], sem_send_info, sem_info, core1_at_y((y + k) % NY)).start()
-
-    @pl.when(core == 0)
-    def _():
-        remote(info_own, info_y.at[mine], sem_send_info, sem_info, sibling).start()
+        remote(info_own, info_y.at[core * NY + y], sem_send_info, sem_info, core1_at_y((y + k) % NY)).start()
+
+    @pl.when(core == 0)
+    def _():
+        remote(info_own, info_y.at[core * NY + y], sem_send_info, sem_info, sibling).start()
 
         def hand_over(r, h):
             ref = hid_pass.at[r, pl.ds(half * h, half)]
@@ -180,7 +192,8 @@
 
     @pl.when(core == 1)
     def _():
-        right, left_ = at_z((z + 1) % NZ), at_z((z + NZ - 1) % NZ)
+        right = [at_z((z + k) % NZ) for k in (1, 2)]
+        left_ = [at_z((z + NZ - k) % NZ) for k in (1, 2)]
 
         def tok_ref(zz, c, h):
             return tok.at[2 * zz + c, pl.ds(quarter * h, quarter)]
@@ -202,52 +215,44 @@
         def info_share(zz):
             remote(info_ref(zz), info_ref(zz), sem_send_sibi, sem_sib_info, sibling).start()
 
+        def tok_send(zz, c, h, where):
+            for there in where:
+                tok_copy(zz, c, h, there).start()
+
+        def info_send(zz, where):
+            for there in where:
+                info_copy(zz, there).start()
+
         for c, h in subs:
             arrived(tok_ref(z, c, h), sem_tok.at[c, h])
-            tok_copy(z, c, h, right).start()
-            tok_copy(z, c, h, left_).start()
+            tok_send(z, c, h, [way[k - 1] for k in HOPS[0] for way in (right, left_)])
             tok_share(z, c, h)
+        info_y[core * NY + y] = info_own[...]
         arrived(info_y.at[pl.ds(0, 2 * NY - 1)], sem_info)
-        info_y[mine] = info_own[...]
         for c in range(2):
-            total_info = info_y[c * NY]
-            for k in range(1, NY):
-                total_info = total_info + info_y[c * NY + k]
-            info[2 * z + c] = total_info
-        info_copy(z, right).start()
-        info_copy(z, left_).start()
+            for i in range(2):
+                info[2 * z + c, NY * i : NY * (i + 1)] = info_y[NY * c : NY * (c + 1), i, :]
+        info_send(z, [way[k - 1] for k in HOPS[0] for way in (right, left_)])
         info_share(z)
 
-        def z_step(d, last):
+        def receive(d):
+            on = HOPS.get(d, ())
             from_left, from_right = (z + NZ - d) % NZ, (z + d) % NZ
+            ways = ((from_left, right, 1), (from_right, left_, 0))
             for c, h in subs:
-                if last < 2 or c == 1:
-                    tok_copy(from_left, c, h, right).wait_recv()
-                    if last == 0 or (last == 1 and c == 1):
-                        tok_copy(from_left, c, h, right).start()
-                    tok_share(from_left, c, h)
-                if last < 2 or c == 0:
-                    tok_copy(from_right, c, h, left_).wait_recv()
-                    if last == 0 or (last == 1 and c == 0):
-                        tok_copy(from_right, c, h, left_).start()
-                    tok_share(from_right, c, h)
-            info_copy(from_left, right).wait_recv()
-            if last < 2:
-                info_copy(from_left, right).start()
-            info_share(from_left)
-            if last < 2:
-                info_copy(from_right, left_).wait_recv()
-                if last == 0:
-                    info_copy(from_right, left_).start()
-                info_share(from_right)
-
-        def z_loop(d, carry):
-            z_step(d, 0)
-            return carry
-
-        lax.fori_loop(1, NZ // 2 - 1, z_loop, 0)
-        z_step(NZ // 2 - 1, 1)
-        z_step(NZ // 2, 2)
+                for source, where, far_core in ways:
+                    if d < REACH or c == far_core:
+                        tok_copy(source, c, h, where[0]).wait_recv()
+                        tok_send(source, c, h, [where[k - 1] for k in on if d + k < REACH or c == far_core])
+                        tok_share(source, c, h)
+            for source, where, far_core in ways:
+                if d < REACH or far_core == 1:
+                    info_copy(source, where[0]).wait_recv()
+                    info_send(source, [where[k - 1] for k in on if d + k < REACH or far_core == 1])
+                    info_share(source)
+
+        for d in ORDER:
+            receive(d)
         local[2].wait()
         arrived(hid.at[pl.ds(0, NY - 1)], sem_sib_h)
 
@@ -265,25 +270,28 @@
     def _():
         arrived(info, sem_sib_info)
 
+    pairs = sources * NY
     both = info[...]
-    hit = both[:, 0:8, :] == expert.astype(F32)
-    named = jnp.sum(jnp.where(hit, 1.0, 0.0), axis=1)
-    gate = jnp.sum(jnp.where(hit, both[:, 8:16, :], 0.0), axis=1)
-    from_row, to_col = iota((128, 128), 0), iota((128, 128), 1)
-    same = from_row // tokens == to_col // tokens
-    before = jnp.where(jnp.logical_and(same, from_row < to_col), 1.0, 0.0).astype(BF16)
+    hit = both[:, 0:NY, :].reshape(pairs, 128) == expert.astype(F32)
+    fold = jnp.where(iota((128, 128), 0) % tokens == iota((128, 128), 1), 1.0, 0.0)
+    named = jnp.dot(jnp.where(hit, 1.0, 0.0).astype(BF16), fold.astype(BF16), preferred_element_type=F32)
+    gate = jnp.dot(
+        jnp.where(hit, both[:, NY : 2 * NY, :].reshape(pairs, 128), 0.0), fold, preferred_element_type=F32,
+        precision=HIGHEST,
+    )
+    before = jnp.where(iota((128, 128), 0) < iota((128, 128), 1), 1.0, 0.0).astype(BF16)
     place = jnp.dot(named.astype(BF16), before, preferred_element_type=F32)
-    target = jnp.where(named > 0.5, place + (cap * iota(named.shape, 0)).astype(F32), -1.0).astype(BF16)
-    count = jnp.sum(named, axis=0, keepdims=True)
-    routed = jnp.dot(
-        jnp.broadcast_to(count, (8, 128)).astype(BF16), jnp.where(same, 1.0, 0.0).astype(BF16),
-        preferred_element_type=F32,
-    )[0:1]
+    target = jnp.where(named > 0.5, place + (cap * (iota(named.shape, 0) // NY)).astype(F32), -1.0)
+    by_replica = jnp.sum(named.reshape(sources, NY, 128), axis=0)
+    routed = jnp.sum(by_replica, axis=1, keepdims=True)
     padded = jnp.floor((routed + (PAD - 1.0)) * (1.0 / PAD)) * PAD
-    total = jnp.sum(padded, axis=1, keepdims=True) * (1.0 / tokens)
-
-    lane_row, lane_col = iota((128, all_tokens), 0), iota((128, all_tokens), 1)
-    own_row = iota((sources, all_tokens), 0) == iota((sources, all_tokens), 1) // tokens
+    total = jnp.sum(padded, axis=0, keepdims=True)
+    repeat = jnp.where(iota((128, all_tokens), 0) == iota((128, all_tokens), 1) % tokens, 1.0, 0.0)
+    target = jnp.dot(target.astype(BF16), repeat.astype(BF16), preferred_element_type=F32)
+    gate = jnp.dot(gate, repeat, preferred_element_type=F32, precision=HIGHEST)
+    own_row = iota((sources, NY, all_tokens), 0) == iota((sources, NY, all_tokens), 2) // tokens
+    target = jnp.sum(jnp.where(own_row, target.reshape(own_row.shape), 0.0), axis=0)
+    gate = jnp.sum(jnp.where(own_row, gate.reshape(own_row.shape), 0.0), axis=0)
     slot_id = iota((slots, all_tokens), 0).astype(F32)
 
     @pl.when(core == 0)
@@ -291,11 +299,7 @@
         arrived(tok, sem_sib)
 
     for r in range(NY):
-        repeat = jnp.where(lane_row == r * tokens + lane_col % tokens, 1.0, 0.0)
-        target_r = jnp.dot(target, repeat.astype(BF16), preferred_element_type=F32)
-        gate_r = jnp.dot(gate, repeat, preferred_element_type=F32, precision=HIGHEST)
-        target_r = jnp.sum(jnp.where(own_row, target_r, 0.0), axis=0, keepdims=True)
-        gate_r = jnp.sum(jnp.where(own_row, gate_r, 0.0), axis=0, keepdims=True)
+        target_r, gate_r = target[r : r + 1], gate[r : r + 1]
         chosen = slot_id == target_r
         gate_col = jnp.sum(jnp.where(chosen, gate_r, 0.0), axis=1, keepdims=True)
         block = tok[:, tokens * r : tokens * (r + 1), :].reshape(all_tokens, width)
@@ -317,50 +321,63 @@
         both_grams = jnp.sum(gram_h * gram_s, axis=0, keepdims=True)
         spread = spread + jnp.sum(both_grams, axis=1, keepdims=True)
 
+    sub = iota((2, 128), 0)
+    vec[dp] = jnp.where(sub == 0, spread, total * (1.0 / NY))
+
+    def to_all(ref, send, recv):
+        for k in (4, 3, 5, 2, 6, 1, 7):
+            for i in range(NX):
+                peer = ((y + k) % NY) * NX + (x + i) % NX
+                remote(ref, ref, send, recv, {"dp": peer}).start()
+        for i in range(1, NX):
+            remote(ref, ref, send, recv, at_x((x + i) % NX)).start()
+
+    to_all(vec.at[dp], sem_send_vec, sem_vec)
+
     summed = part[:, x].reshape(NY * owned, width)
     for k in (1, 3, 2):
         peer = (x + k) % NX
         arrived(recv_x.at[peer], sem_x.at[peer])
         summed = summed + recv_x[peer].astype(F32)
-    own[...] = summed
 
     power = jnp.sum(jnp.sum(summed * summed, axis=0, keepdims=True), axis=1, keepdims=True)
-    sub = iota((8, 128), 0)
-    vec[dp] = jnp.where(
-        sub == 0, power, jnp.where(sub == 1, spread, jnp.where(sub == 2, total * (1.0 / NY), 0.0))
-    )
-    for k in (4, 3, 5, 2, 6, 1, 7):
-        for i in range(NX):
-            peer = ((y + k) % NY) * NX + (x + i) % NX
-            remote(vec.at[dp], vec.at[dp], sem_send_vec, sem_vec, {"dp": peer}).start()
-    for i in range(1, NX):
-        remote(vec.at[dp], vec.at[dp], sem_send_vec, sem_vec, at_x((x + i) % NX)).start()
+    norms[dp] = jnp.broadcast_to(power, (1, 128))
+    to_all(norms.at[dp], sem_send_norms, sem_norms)
+    for k in range(NY):
+        piece = summed[owned * k : owned * (k + 1), :]
+        own[k] = jnp.concatenate([piece[:, : width // 2], piece[:, width // 2 :]], axis=0).astype(BF16)
     for k in (4, 3, 5, 2, 6, 1, 7):
         peer = (y + k) % NY
-        remote(own.at[rows(peer, owned)], relay.at[y], sem_send_relay, sem_relay, at_y(peer)).start()
-    relay[y] = own[rows(y, owned), :]
+        remote(own.at[peer], relay.at[y], sem_send_relay, sem_relay, at_y(peer)).start()
+    relay[y] = own[y]
     local[3].wait()
     local[4].wait()
-    arrived(relay.at[pl.ds(0, NY - 1)], sem_relay)
     arrived(vec.at[pl.ds(0, NX * NY - 1)], sem_vec)
     scalars = vec[0]
     for k in range(1, NX * NY):
         scalars = scalars + vec[k]
-    power, spread, total = scalars[0:1, 0:1], scalars[1:2, 0:1], scalars[2:3, 0:1]
+    spread, total = scalars[0:1, 0:1], scalars[1:2, 0:1]
+    arrived(relay.at[pl.ds(0, NY - 1)], sem_relay)
+    for k in range(NY):
+        rows_k = relay[k].astype(F32)
+        for h in range(2):
+            cols = pl.ds(width * k + width // 2 * h, width // 2)
+            mean = rows_k[owned * h : owned * (h + 1)] / total
+            first = 0.9 * mom1[:, cols] + 0.1 * mean
+            second = 0.95 * mom2[:, cols] + 0.05 * mean * mean
+            mom1[:, cols] = (first / (1.0 - 0.9**ADAM_STEP)) / (
+                jnp.sqrt(second / (1.0 - 0.95**ADAM_STEP)) + 1e-08
+            )
+    arrived(norms.at[pl.ds(0, NX * NY - 1)], sem_norms)
+    power = norms[0]
+    for k in range(1, NX * NY):
+        power = power + norms[k]
+    power = power[:, 0:1]
     replicas = float(NX * NY)
     noise = total * spread / (replicas * power + 1e-06)
     lr_scale = noise / (noise + total / replicas)
     lr_out[0] = lr_scale[0, 0]
-    for k in range(NY):
-        cols = pl.ds(width * k, width)
-        mean = relay[k] / total
-        first = 0.9 * mom1[:, cols] + 0.1 * mean
-        second = 0.95 * mom2[:, cols] + 0.05 * mean * mean
-        out[0, :, cols] = (
-            -lr_scale
-            * (first / (1.0 - 0.9**ADAM_STEP))
-            / (jnp.sqrt(second / (1.0 - 0.95**ADAM_STEP)) + 1e-08)
-        )
+    out[0] = -lr_scale * mom1[...]
 
     tok_flat = tok.at[0, pl.ds(0, tokens * (NY - 1))]
     left(tok_flat, sem_send_tok)
@@ -369,6 +386,7 @@
         left(send_x.at[(x + k) % NX], sem_send_x.at[k])
     left(relay.at[pl.ds(0, NY - 1)], sem_send_relay)
     left(vec.at[pl.ds(0, NX * NY - 1)], sem_send_vec)
+    left(norms.at[pl.ds(0, NX * NY - 1)], sem_send_norms)
 
     @pl.when(core == 0)
     def _():
@@ -406,9 +424,10 @@
         out_specs=(vmem, pl.BlockSpec(memory_space=pltpu.SMEM)),
         scratch_shapes=[
             pltpu.VMEM((2 * NZ, NY * tokens, width), BF16),
-            pltpu.VMEM((2 * NZ, 16, 128), F32),
-            pltpu.VMEM((2 * NY, 16, 128), F32),
-            pltpu.VMEM((16, 128), F32),
+            pltpu.VMEM((2 * NZ, 2 * NY, 128), F32),
+            pltpu.VMEM((2 * NY, 2, 128), F32),
+            pltpu.VMEM((2, 128), F32),
+            pltpu.VMEM(out_grad.shape[1:], BF16),
             pltpu.VMEM((NY, slots, units), BF16),
             pltpu.VMEM((NY, slots, units), BF16),
             pltpu.VMEM((units, NY * slots), BF16),
@@ -416,14 +435,15 @@
             pltpu.VMEM((NY, NX, owned, width), F32),
             pltpu.VMEM((NX, NY * owned, width), BF16),
             pltpu.VMEM((NX, NY * owned, width), BF16),
-            pltpu.VMEM((NY * owned, width), F32),
-            pltpu.VMEM((NY, owned, width), F32),
-            pltpu.VMEM((NX * NY, 8, 128), F32),
+            pltpu.VMEM((NY, 2 * owned, width // 2), BF16),
+            pltpu.VMEM((NY, 2 * owned, width // 2), BF16),
+            pltpu.VMEM((NX * NY, 2, 128), F32),
+            pltpu.VMEM((NX * NY, 1, 128), F32),
             pltpu.VMEM(first_prev.shape[1:], F32),
             pltpu.VMEM(first_prev.shape[1:], F32),
             pltpu.VMEM(routes.shape, jnp.int32),
             pltpu.VMEM(routes.shape, F32),
-            dma((5,)),
+            dma((6,)),
             dma((2, 2)),
             dma,
             dma,
@@ -444,6 +464,8 @@
             dma,
             dma((NX,)),
             dma((NX,)),
+            dma,
+            dma,
             dma,
             dma,
             dma,

time: 78 us -> 70.1 us (0.90)
  Pallas kernels: 73.8 us -> 65.9 us
    pallas_call x1, Pallas kernels: 73.8 us -> 65.9 us  [on_device(): pl.pallas_call(kernel, out_shape=(jax.ShapeDtypeStruct(first_prev.shape,...]
where the time goes in v3:
time: 70.1 us; the launch traced here: 69.9 us
  Pallas kernels  65.9 us (94%)
  between operations  2.4 us (3%)
  local copies, waits for them, and re-layouts  1.62 us (2%)
    pallas_call x1, Pallas kernels, on_device(): pl.pallas_call(kernel, out_shape=(jax.ShapeDtypeStruct(first_prev.shape,...  65.9 us
    unnamed x1, local copies, waits for them, and re-layouts  1.62 us

profile of v3, /device:TPU:1, one launch (start us, length us, event | category | flops | bytes accessed | tf_op | source)
XLA Modules:
  0.0 69.9 jit_solution(7130677103597019103)
XLA Ops:
  0.6 65.9 %shard_map.77 = (f32[1,24,2048]{2,1,0:T(8,128)}, f32[1]{0:T(128)}) custom-call(bf16[1,16,2048]{2,1,0:T(8,128)(2,1)} %grads.1, s32[1,8,16]{2,1,0:T(8,128)} %bitcast.2, f32[1,8,16]{2,1,0:T(8,128)} %bitcast.3, bf16[1,1,160,768]{3,2,1,0:T(8,128)(2,1)} %hidden.1, f32[1,24,2048]{2,1,0:T(8,128)} %first_prev.1, f32[1,24,2048]{2,1,0:T(8,128)} %second_prev.1), custom_call_target="tpu_custom_call" | custom-call | tf_op jit(solution)/shard_map/pallas_call | solution.py:417
  66.5 1.6 %copy.10 = f32[1,24,2048]{2,1,0:T(8,128)} copy(f32[1,24,2048]{2,1,0:T(8,128)} %get-tuple-element.4) | data formatting | bytes 393216

commit v4 on v3

--- a/solution.py
+++ b/solution.py
@@ -10,6 +10,7 @@
 MESH = pl.DeviceIdType.MESH
 NX, NY, NZ = 4, 8, 16
 REACH = NZ // 2
+NEAR_FIRST = (1, 7, 6, 4, 5, 3, 2)
 HOPS = {0: (2, 1), 2: (2, 1), 4: (2, 1), 6: (2, 1)}
 ORDER = (2, 1, 4, 3, 6, 5, 8, 7)
 HIGHEST = lax.Precision.HIGHEST
@@ -23,7 +24,7 @@
 
 def kernel(
     grads, routes_in, gates_in, hidden, first_prev, second_prev,
-    out, lr_out,
+    ratio, lr_out,
     tok, info, info_y, info_own, grads_here, hid, hid_pass, hid_t, sent, part, send_x, recv_x, own, relay, vec, norms, mom1, mom2,
     routes, gates,
     sem_local, sem_tok, sem_send_tok, sem_info, sem_send_info,
@@ -121,24 +122,25 @@
     def _():
         pl.semaphore_wait(barrier, NX * NY - 1 + NY)
 
-    my_rows = rows(y, tokens)
     local[5].wait()
-    for k in range(1, NY):
-        peer = (y + k) % NY
+
+    def token_send(k, where):
+        place = (1 - k) % NY
         remote(
-            grads_here.at[:, columns(peer)], tok.at[expert, my_rows], sem_send_tok, sem_tok.at[core, y // 4],
-            core1_at_y(peer),
+            grads_here.at[:, columns((y + k) % NY)], tok.at[expert, pl.ds(place * tokens, tokens)], sem_send_tok,
+            sem_tok.at[core, 2 * place // NY], where,
         ).start()
 
     @pl.when(core == 0)
     def _():
-        remote(
-            grads_here.at[:, columns(y)], tok.at[expert, my_rows], sem_send_tok, sem_tok.at[core, y // 4], sibling
-        ).start()
+        token_send(0, sibling)
+
+    for k in NEAR_FIRST:
+        token_send(k, core1_at_y((y + k) % NY))
 
     @pl.when(core == 1)
     def _():
-        pltpu.make_async_copy(grads_here.at[:, columns(y)], tok.at[expert, my_rows], sem_tok.at[core, y // 4]).start()
+        pltpu.make_async_copy(grads_here.at[:, columns(y)], tok.at[expert, pl.ds(tokens, tokens)], sem_tok.at[core, 0]).start()
         remote(hidden.at[0, 0], hid_pass.at[y], sem_send_hand, sem_hand, sibling).start()
 
     up, down = at_y((y + 1) % NY), at_y((y + NY - 1) % NY)
@@ -155,12 +157,14 @@
             hid_copy(0, y, h, up, True).start()
             hid_copy(0, y, h, down, True).start()
 
-    for k in range(1, NY):
-        remote(info_own, info_y.at[core * NY + y], sem_send_info, sem_info, core1_at_y((y + k) % NY)).start()
-
-    @pl.when(core == 0)
-    def _():
-        remote(info_own, info_y.at[core * NY + y], sem_send_info, sem_info, sibling).start()
+    for k in NEAR_FIRST:
+        remote(
+            info_own, info_y.at[core * NY + (1 - k) % NY], sem_send_info, sem_info, core1_at_y((y + k) % NY)
+        ).start()
+
+    @pl.when(core == 0)
+    def _():
+        remote(info_own, info_y.at[core * NY + 1], sem_send_info, sem_info, sibling).start()
 
         def hand_over(r, h):
             ref = hid_pass.at[r, pl.ds(half * h, half)]
@@ -188,7 +192,7 @@
                             hand_over(above, h)
         local[2].wait()
 
-    subs = ((1, 0), (1, 1), (0, 0), (0, 1))
+    subs = ((1, 0), (0, 0), (1, 1), (0, 1))
 
     @pl.when(core == 1)
     def _():
@@ -227,7 +231,7 @@
             arrived(tok_ref(z, c, h), sem_tok.at[c, h])
             tok_send(z, c, h, [way[k - 1] for k in HOPS[0] for way in (right, left_)])
             tok_share(z, c, h)
-        info_y[core * NY + y] = info_own[...]
+        info_y[core * NY + 1] = info_own[...]
         arrived(info_y.at[pl.ds(0, 2 * NY - 1)], sem_info)
         for c in range(2):
             for i in range(2):
@@ -256,15 +260,20 @@
         local[2].wait()
         arrived(hid.at[pl.ds(0, NY - 1)], sem_sib_h)
 
+    def hid_at(place):
+        return (y + NY - 1 + place) % NY
+
     for k in range(NY * slots // 128):
         first, last = 128 * k // slots, (128 * k + 127) // slots
         begin = 128 * k - first * slots
         if first == last:
-            piece = hid[first, begin : begin + 128, :]
+            piece = hid[hid_at(first), begin : begin + 128, :]
         else:
             cut = slots - begin
-            piece = jnp.concatenate([hid[first, begin:slots, :], hid[last, 0 : 128 - cut, :]], axis=0)
-        hid_t[:, 128 * k : 128 * (k + 1)] = piece.T
+            piece = jnp.concatenate([hid[hid_at(first), begin:slots, :], hid[hid_at(last), 0 : 128 - cut, :]], axis=0)
+        piece = piece.astype(F32).T.reshape(NY, NX, owned, 128)
+        for i in range(NX):
+            hid_t[i, :, 128 * k : 128 * (k + 1)] = piece[:, i].reshape(NY * owned, 128).astype(BF16)
 
     @pl.when(core == 0)
     def _():
@@ -306,17 +315,27 @@
         picked = jnp.dot(jnp.where(chosen, 1.0, 0.0).astype(BF16), block, preferred_element_type=F32)
         sent[slots * r : slots * (r + 1), :] = (picked * gate_col).astype(BF16)
 
-    part[...] = jnp.dot(hid_t[...], sent[...], preferred_element_type=F32).reshape(NY, NX, owned, width)
-    for k in (2, 1, 3):
+    def x_send(k, rows_of):
         peer = (x + k) % NX
-        send_x[peer] = part[:, peer].reshape(NY * owned, width).astype(BF16)
+        send_x[peer] = rows_of.astype(BF16)
         remote(send_x.at[peer], recv_x.at[x], sem_send_x.at[k], sem_x.at[x], at_x(peer)).start()
+
+    for pair in ((2, 1), (3, 0)):
+        hid_rows = jnp.concatenate([hid_t[(x + k) % NX] for k in pair], axis=0)
+        product = jnp.dot(hid_rows, sent[...], preferred_element_type=F32)
+        for i, k in enumerate(pair):
+            rows_of = product[NY * owned * i : NY * owned * (i + 1)]
+            if k:
+                x_send(k, rows_of)
+            else:
+                part[...] = rows_of
 
     over = (((1,), (1,)), ((), ()))
     spread = jnp.zeros((1, 1), F32)
     for r in range(NY):
         sent_r = sent[slots * r : slots * (r + 1), :]
-        gram_h = lax.dot_general(hid[r], hid[r], over, preferred_element_type=F32)
+        hid_r = hid[hid_at(r)]
+        gram_h = lax.dot_general(hid_r, hid_r, over, preferred_element_type=F32)
         gram_s = lax.dot_general(sent_r, sent_r, over, preferred_element_type=F32)
         both_grams = jnp.sum(gram_h * gram_s, axis=0, keepdims=True)
         spread = spread + jnp.sum(both_grams, axis=1, keepdims=True)
@@ -334,7 +353,7 @@
 
     to_all(vec.at[dp], sem_send_vec, sem_vec)
 
-    summed = part[:, x].reshape(NY * owned, width)
+    summed = part[...]
     for k in (1, 3, 2):
         peer = (x + k) % NX
         arrived(recv_x.at[peer], sem_x.at[peer])
@@ -368,6 +387,8 @@
             mom1[:, cols] = (first / (1.0 - 0.9**ADAM_STEP)) / (
                 jnp.sqrt(second / (1.0 - 0.95**ADAM_STEP)) + 1e-08
             )
+    write = pltpu.make_async_copy(mom1, ratio.at[0], sem_local.at[0])
+    write.start()
     arrived(norms.at[pl.ds(0, NX * NY - 1)], sem_norms)
     power = norms[0]
     for k in range(1, NX * NY):
@@ -377,8 +398,8 @@
     noise = total * spread / (replicas * power + 1e-06)
     lr_scale = noise / (noise + total / replicas)
     lr_out[0] = lr_scale[0, 0]
-    out[0] = -lr_scale * mom1[...]
-
+
+    write.wait()
     tok_flat = tok.at[0, pl.ds(0, tokens * (NY - 1))]
     left(tok_flat, sem_send_tok)
     left(info_y.at[pl.ds(0, NY - 1)], sem_send_info)
@@ -413,15 +434,14 @@
     owned = units // (NX * NY)
     dma = pltpu.SemaphoreType.DMA
     hbm = pl.BlockSpec(memory_space=pltpu.HBM)
-    vmem = pl.BlockSpec(memory_space=pltpu.VMEM)
-    return pl.pallas_call(
+    ratio, lr_scale = pl.pallas_call(
         kernel,
         out_shape=(
             jax.ShapeDtypeStruct(first_prev.shape, F32),
             jax.ShapeDtypeStruct((1,), F32),
         ),
         in_specs=[hbm] * 6,
-        out_specs=(vmem, pl.BlockSpec(memory_space=pltpu.SMEM)),
+        out_specs=(hbm, pl.BlockSpec(memory_space=pltpu.SMEM)),
         scratch_shapes=[
             pltpu.VMEM((2 * NZ, NY * tokens, width), BF16),
             pltpu.VMEM((2 * NZ, 2 * NY, 128), F32),
@@ -430,9 +450,9 @@
             pltpu.VMEM(out_grad.shape[1:], BF16),
             pltpu.VMEM((NY, slots, units), BF16),
             pltpu.VMEM((NY, slots, units), BF16),
-            pltpu.VMEM((units, NY * slots), BF16),
+            pltpu.VMEM((NX, NY * owned, NY * slots), BF16),
             pltpu.VMEM((NY * slots, width), BF16),
-            pltpu.VMEM((NY, NX, owned, width), F32),
+            pltpu.VMEM((NY * owned, width), F32),
             pltpu.VMEM((NX, NY * owned, width), BF16),
             pltpu.VMEM((NX, NY * owned, width), BF16),
             pltpu.VMEM((NY, 2 * owned, width // 2), BF16),
@@ -475,6 +495,7 @@
             collective_id=0, has_side_effects=True, vmem_limit_bytes=60 * 1024 * 1024
         ),
     )(out_grad, routes, gate_probs, hidden, first_prev, second_prev)
+    return -lr_scale[0] * ratio, lr_scale
 
 
 def solution(mesh):

time: 70.1 us -> 69.6 us (level)
  other arithmetic: 0 us -> 1.62 us
  local copies, waits for them, and re-layouts: 1.62 us -> 0 us
  Pallas kernels: 65.9 us -> 64.7 us
    mul x0 -> x1, other arithmetic: none -> 1.62 us  [on_device(): return (-lr_scale[0] * ratio, lr_scale)]
    unnamed x1 -> x0, local copies, waits for them, and re-layouts: 1.62 us -> none
    pallas_call x1, Pallas kernels: 65.9 us -> 64.7 us  [on_device(): pl.pallas_call(kernel, out_shape=(jax.ShapeDtypeStruct(first_prev.shape,...]
where the time goes in v4:
time: 69.6 us; the launch traced here: 69.4 us
  Pallas kernels  64.7 us (93%)
  between operations  3.04 us (4%)
  other arithmetic  1.62 us (2%)
    pallas_call x1, Pallas kernels, on_device(): pl.pallas_call(kernel, out_shape=(jax.ShapeDtypeStruct(first_prev.shape,...  64.7 us
    mul x1, other arithmetic, on_device(): return (-lr_scale[0] * ratio, lr_scale)  1.62 us

profile of v4, /device:TPU:1, one launch (start us, length us, event | category | flops | bytes accessed | tf_op | source)
XLA Modules:
  0.0 69.4 jit_solution(10080130134926074211)
XLA Ops:
  0.6 64.7 %shard_map.77 = (f32[1,24,2048]{2,1,0:T(8,128)}, f32[1]{0:T(128)}) custom-call(bf16[1,16,2048]{2,1,0:T(8,128)(2,1)} %grads.1, s32[1,8,16]{2,1,0:T(8,128)} %bitcast.3, f32[1,8,16]{2,1,0:T(8,128)} %bitcast.4, bf16[1,1,160,768]{3,2,1,0:T(8,128)(2,1)} %hidden.1, f32[1,24,2048]{2,1,0:T(8,128)} %first_prev.1, f32[1,24,2048]{2,1,0:T(8,128)} %second_prev.1), custom_call_target="tpu_custom_call" | custom-call | tf_op jit(solution)/shard_map/pallas_call | solution.py:437
  66.0 1.6 %broadcast_multiply_fusion = f32[1,24,2048]{2,1,0:T(8,128)} fusion(f32[1,24,2048]{2,1,0:T(8,128)} %get-tuple-element.5, f32[]{:T(128)} %bitcast.2), kind=kLoop, calls=%fused_computation | loop fusion | flops 49152 | bytes 393220 | tf_op jit(solution)/shard_map/mul | solution.py:498

commit v5 on v4

--- a/solution.py
+++ b/solution.py
@@ -192,7 +192,7 @@
                             hand_over(above, h)
         local[2].wait()
 
-    subs = ((1, 0), (0, 0), (1, 1), (0, 1))
+    subs = ((0, 0), (1, 0), (0, 1), (1, 1))
 
     @pl.when(core == 1)
     def _():
@@ -234,8 +234,8 @@
         info_y[core * NY + 1] = info_own[...]
         arrived(info_y.at[pl.ds(0, 2 * NY - 1)], sem_info)
         for c in range(2):
-            for i in range(2):
-                info[2 * z + c, NY * i : NY * (i + 1)] = info_y[NY * c : NY * (c + 1), i, :]
+            both_rows = [info_y[NY * c : NY * (c + 1), i, :] for i in range(2)]
+            info[2 * z + c] = jnp.concatenate(both_rows, axis=0).astype(BF16)
         info_send(z, [way[k - 1] for k in HOPS[0] for way in (right, left_)])
         info_share(z)
 
@@ -280,7 +280,7 @@
         arrived(info, sem_sib_info)
 
     pairs = sources * NY
-    both = info[...]
+    both = info[...].astype(F32)
     hit = both[:, 0:NY, :].reshape(pairs, 128) == expert.astype(F32)
     fold = jnp.where(iota((128, 128), 0) % tokens == iota((128, 128), 1), 1.0, 0.0)
     named = jnp.dot(jnp.where(hit, 1.0, 0.0).astype(BF16), fold.astype(BF16), preferred_element_type=F32)
@@ -444,7 +444,7 @@
         out_specs=(hbm, pl.BlockSpec(memory_space=pltpu.SMEM)),
         scratch_shapes=[
             pltpu.VMEM((2 * NZ, NY * tokens, width), BF16),
-            pltpu.VMEM((2 * NZ, 2 * NY, 128), F32),
+            pltpu.VMEM((2 * NZ, 2 * NY, 128), BF16),
             pltpu.VMEM((2 * NY, 2, 128), F32),
             pltpu.VMEM((2, 128), F32),
             pltpu.VMEM(out_grad.shape[1:], BF16),

time: 69.6 us -> 68.6 us (0.986)
  Pallas kernels: 64.7 us -> 63.7 us
    pallas_call x1, Pallas kernels: 64.7 us -> 63.7 us  [on_device(): pl.pallas_call(kernel, out_shape=(jax.ShapeDtypeStruct(first_prev.shape,...]
where the time goes in v5:
time: 68.6 us; the launch traced here: 68.3 us
  Pallas kernels  63.7 us (93%)
  between operations  3.04 us (4%)
  other arithmetic  1.62 us (2%)
    pallas_call x1, Pallas kernels, on_device(): pl.pallas_call(kernel, out_shape=(jax.ShapeDtypeStruct(first_prev.shape,...  63.7 us
    mul x1, other arithmetic, on_device(): return (-lr_scale[0] * ratio, lr_scale)  1.62 us

profile of v5, /device:TPU:1, one launch (start us, length us, event | category | flops | bytes accessed | tf_op | source)
XLA Modules:
  0.0 68.3 jit_solution(9649557853385289476)
XLA Ops:
  0.6 63.7 %shard_map.77 = (f32[1,24,2048]{2,1,0:T(8,128)}, f32[1]{0:T(128)}) custom-call(bf16[1,16,2048]{2,1,0:T(8,128)(2,1)} %grads.1, s32[1,8,16]{2,1,0:T(8,128)} %bitcast.3, f32[1,8,16]{2,1,0:T(8,128)} %bitcast.4, bf16[1,1,160,768]{3,2,1,0:T(8,128)(2,1)} %hidden.1, f32[1,24,2048]{2,1,0:T(8,128)} %first_prev.1, f32[1,24,2048]{2,1,0:T(8,128)} %second_prev.1), custom_call_target="tpu_custom_call" | custom-call | tf_op jit(solution)/shard_map/pallas_call | solution.py:437
  64.9 1.6 %broadcast_multiply_fusion = f32[1,24,2048]{2,1,0:T(8,128)} fusion(f32[1,24,2048]{2,1,0:T(8,128)} %get-tuple-element.5, f32[]{:T(128)} %bitcast.2), kind=kLoop, calls=%fused_computation | loop fusion | flops 49152 | bytes 393220 | tf_op jit(solution)/shard_map/mul | solution.py:498
